TPU v7x, 32 devices: a whole 2x2x4 slice. The times are simulated.
32 devices in a mesh: tm: 8 (over z, core), trace: 4 (over y, x).
Axes of the slice: x: 2, y: 2, z: 4, core: 2. Of those that a mesh axis runs over, the one named last changes fastest.
Arguments:
- observed: bfloat16 [64, 4096], P('trace', 'tm'), may hold values from -32 to 32
- sampled: int32 [64, 4096], P('trace', 'tm'), may hold values 0 or 1
- probes: bfloat16 [256, 64, 128], P(None, 'trace'), may hold values from -0.046875 to 0.046875
Outputs:
- completed: float32 [64, 4096], P('trace', 'tm')
All inputs are finite; a program needn't handle non-finite values. No bound on the sum of `sampled` on one device may be relied on, other than what follows from the above.
Results may differ from a plain program's by a relative error of at most 0.0004.
Values may be sent and summed in bfloat16 or wider, within the bound.
A program may use at most 64 MiB of HBM per device.

v0:
```python
import functools

import jax
import jax.numpy as jnp
from jax import lax
from jax.experimental import pallas as pl
from jax.experimental.pallas import tpu as pltpu
from jax.sharding import PartitionSpec as P

LANES = 128
SUB = 8
BF = jnp.bfloat16
F32 = jnp.float32


def nt(a, b):
    return lax.dot_general(a, b, (((1,), (1,)), ((), ())), preferred_element_type=F32)


def nn(a, b):
    return lax.dot_general(a, b, (((1,), (0,)), ((), ())), preferred_element_type=F32)


def split3(x):
    hi = x.astype(BF)
    rest = x - hi.astype(F32)
    mid = rest.astype(BF)
    low = (rest - mid.astype(F32)).astype(BF)
    return hi, mid, low


def inverse_factor(gram):
    size = gram.shape[0]
    blocks = size // SUB
    rows = lax.broadcasted_iota(jnp.int32, (SUB, size), 0)
    lanes = lax.broadcasted_iota(jnp.int32, (SUB, size), 1)
    left = [gram[SUB * a : SUB * (a + 1)] for a in range(blocks)]
    right = [jnp.where(lanes == rows + SUB * a, 1.0, 0.0).astype(F32) for a in range(blocks)]
    scales = []
    for a0 in range(blocks):
        wide = {
            a: [jnp.broadcast_to(left[a][:, SUB * a0 + q : SUB * a0 + q + 1], (SUB, size)) for q in range(SUB)]
            for a in range(a0, blocks)
        }
        scale = jnp.zeros((SUB, size), F32)
        for s in range(SUB):
            pivot = wide[a0][s][s : s + 1]
            inverse = 1.0 / pivot
            scale = jnp.where(rows == s, pivot, scale)
            row_left = left[a0][s : s + 1] * inverse
            row_right = right[a0][s : s + 1] * inverse
            row_wide = {q: wide[a0][q][s : s + 1] * inverse for q in range(s + 1, SUB)}
            for a in range(a0, blocks):
                factor = wide[a][s]
                if a == a0:
                    factor = jnp.where(rows > s, factor, 0.0)
                left[a] = left[a] - factor * row_left
                right[a] = right[a] - factor * row_right
                for q in range(s + 1, SUB):
                    wide[a][q] = wide[a][q] - factor * row_wide[q]
        scales.append(lax.rsqrt(scale))
    return jnp.concatenate([right[a] * scales[a] for a in range(blocks)], axis=0)


def kernel(
    n_tm, n_tr,
    observed, sampled, probes, out,
    data, halo, slices, windows, rolled, probes_t, part, parts_in, sketch, flat,
    hankel, spread, est_out, est_in,
    halo_sems, win_send, win_recv, part_send, part_recv,
    z_send, z_recv, x_send, x_recv, c_send, c_recv, est_send, est_recv,
):
    tm = lax.axis_index("tm")
    tr = lax.axis_index("trace")
    n_z = n_tm // 2
    z = tm // 2
    core = lax.rem(tm, 2)
    traces, width = data.shape
    own = traces // n_tm
    groups, contract, probe_count = probes.shape
    taps = groups * LANES
    chunks = width // LANES
    total = n_tm * chunks
    samples = n_tm * width
    share = part.shape[0] // n_tr

    def copy(src, dst, send, recv, **to):
        return pltpu.make_async_remote_copy(
            src_ref=src, dst_ref=dst, send_sem=send, recv_sem=recv,
            device_id=to, device_id_type=pl.DeviceIdType.MESH,
        )

    barrier = pltpu.get_barrier_semaphore()
    for off in range(1, n_tm):
        pl.semaphore_signal(barrier, inc=1, device_id={"tm": lax.rem(tm + off, n_tm)}, device_id_type=pl.DeviceIdType.MESH)
    for off in range(1, n_tr):
        pl.semaphore_signal(barrier, inc=1, device_id={"trace": lax.rem(tr + off, n_tr)}, device_id_type=pl.DeviceIdType.MESH)

    masked = jnp.where(sampled[...] == 1, observed[...].astype(F32), 0.0)
    data[...] = masked.astype(BF)
    for i in range(n_tm):
        slices[i] = masked[own * i : own * (i + 1)]
    pl.semaphore_wait(barrier, n_tm + n_tr - 2)

    pending = []
    before = lax.rem(tm + n_tm - 1, n_tm)
    halo_copy = copy(data.at[:, pl.ds(0, taps)], halo, halo_sems.at[0], halo_sems.at[1], tm=before)
    halo_copy.start()
    pending.append(halo_copy)
    for off in range(1, n_tm):
        dst = lax.rem(tm + off, n_tm)
        c = copy(slices.at[dst], windows.at[tm], win_send.at[off], win_recv.at[off], tm=dst)
        c.start()
        pending.append(c)
    windows[tm] = slices[tm]

    with jax.named_scope("probes_transposed"):
        for g in range(groups):
            probes_t[probe_count * g : probe_count * (g + 1), :] = probes[g].T

    halo_copy.wait_recv()
    with jax.named_scope("sketch_part"):
        tail = jnp.where(tm < n_tm - 1, halo[...].astype(F32), 0.0)
        extended = jnp.concatenate([masked, tail], axis=1)
        reach = extended.shape[1]
        keep = rolled.shape[1]
        for j in range(LANES):
            moved = pltpu.roll(extended, reach - j, 1) if j else extended
            rolled[traces * j : traces * (j + 1), :] = moved[:, :keep].astype(BF)
        both = nn(probes_t[...], rolled[...])
        for b in range(chunks):
            block = both[:probe_count, LANES * b : LANES * (b + 1)]
            for g in range(1, groups):
                block = block + both[probe_count * g : probe_count * (g + 1), LANES * (b + g) : LANES * (b + g + 1)]
            part[probe_count * b : probe_count * (b + 1), :] = block.astype(BF)

    part_copies = []
    for off in range(1, n_tr):
        dst = lax.rem(tr + off, n_tr)
        c = copy(
            part.at[pl.ds(pl.multiple_of(dst * share, share), share), :], parts_in.at[tr],
            part_send.at[off], part_recv.at[off], trace=dst,
        )
        c.start()
        pending.append(c)
    summed = part[pl.ds(pl.multiple_of(tr * share, share), share), :].astype(F32)
    for off in range(1, n_tr):
        src = lax.rem(tr + n_tr - off, n_tr)
        copy(
            part.at[pl.ds(0, share), :], parts_in.at[src], part_send.at[off], part_recv.at[off], trace=src
        ).wait_recv()
        summed = summed + parts_in[src].astype(F32)
    sketch[tm, pl.ds(pl.multiple_of(tr * share, share), share), :] = summed.astype(BF)

    def place(zo, ro, parity):
        t = lax.rem(z + n_z - zo, n_z) * 2 + parity
        r = lax.rem(tr + n_tr - ro, n_tr)
        return sketch.at[t, pl.ds(pl.multiple_of(r * share, share), share), :]

    def along_z(zo):
        here = place(0, 0, core)
        return copy(here, here, z_send.at[zo], z_recv.at[zo], tm=lax.rem(z + zo, n_z) * 2 + core)

    def across(zo, ro):
        here = place(zo, 0, core)
        return copy(here, here, x_send.at[zo, ro], x_recv.at[zo, ro], trace=lax.rem(tr + ro, n_tr))

    def to_sibling(zo, ro):
        here = place(zo, ro, core)
        return copy(here, here, c_send.at[zo, ro], c_recv.at[zo, ro], tm=z * 2 + 1 - core)

    def go(c):
        c.start()
        pending.append(c)

    def arrived(zo, ro, send, recv, parity):
        there = place(zo, ro, parity)
        copy(there, there, send, recv, tm=z * 2 + 1 - core).wait_recv()

    for zo in range(1, n_z):
        go(along_z(zo))
    for ro in range(1, n_tr):
        go(across(0, ro))
    go(to_sibling(0, 0))

    for off in range(1, n_tm):
        src = lax.rem(tm + n_tm - off, n_tm)
        copy(slices.at[src], windows.at[src], win_send.at[off], win_recv.at[off], tm=src).wait_recv()
    with jax.named_scope("hankel"):
        rows = lax.broadcasted_iota(jnp.int32, (LANES, LANES), 0)
        lanes = lax.broadcasted_iota(jnp.int32, (LANES, LANES), 1)
        for c in range(own):
            ahead = None
            for m in range(total + groups - 2, -1, -1):
                if m < total:
                    t, b = m // chunks, m % chunks
                    line = windows[t, c : c + 1, LANES * b : LANES * (b + 1)]
                    now = pltpu.roll(jnp.broadcast_to(line, (LANES, LANES)), 1, 1, stride=1, stride_axis=0)
                else:
                    now = jnp.zeros((LANES, LANES), F32)
                if ahead is None:
                    ahead = jnp.zeros((LANES, LANES), F32)
                hankel[LANES * c : LANES * (c + 1), LANES * m : LANES * (m + 1)] = jnp.where(
                    lanes <= rows, now, ahead
                ).astype(BF)
                ahead = now

    for zo in range(1, n_z):
        arrived(zo, 0, z_send.at[zo], z_recv.at[zo], core)
        for ro in range(1, n_tr):
            go(across(zo, ro))
        go(to_sibling(zo, 0))
    for zo in range(n_z):
        for ro in range(1, n_tr):
            arrived(zo, ro, x_send.at[zo, ro], x_recv.at[zo, ro], core)
            go(to_sibling(zo, ro))
    for zo in range(n_z):
        for ro in range(n_tr):
            arrived(zo, ro, c_send.at[zo, ro], c_recv.at[zo, ro], 1 - core)

    with jax.named_scope("gram"):
        for t in range(n_tm):
            for b in range(chunks):
                m = t * chunks + b
                flat[:, LANES * m : LANES * (m + 1)] = sketch[t, probe_count * b : probe_count * (b + 1), :]
        gram = nt(flat[...], flat[...])
    with jax.named_scope("inverse_factor"):
        hi, mid, low = split3(inverse_factor(gram))
    with jax.named_scope("basis"):
        for g in range(groups):
            rows_g = slice(probe_count * g, probe_count * (g + 1))
            if g:
                spread[rows_g, : LANES * g] = jnp.zeros((probe_count, LANES * g), BF)
            if g < groups - 1:
                spread[rows_g, LANES * (total + g) :] = jnp.zeros((probe_count, LANES * (groups - 1 - g)), BF)
        for t in range(n_tm):
            piece = flat[:, width * t : width * (t + 1)]
            basis = (nn(low, piece) + nn(mid, piece) + nn(hi, piece)).astype(BF)
            for g in range(groups):
                spread[probe_count * g : probe_count * (g + 1), width * t + LANES * g : width * (t + 1) + LANES * g] = basis
    with jax.named_scope("coefs"):
        coefs = nt(hankel[...], spread[...]).astype(BF)
        flip = jnp.where(lanes + rows == LANES - 1, 1.0, 0.0).astype(BF)
        coefs = jnp.concatenate(
            [nn(flip, coefs[LANES * c : LANES * (c + 1)]).astype(BF) for c in range(own)], axis=0
        )
    with jax.named_scope("antidiagonals"):
        carry = [jnp.zeros((SUB, LANES), F32) for _ in range(own)]
        for t in range(n_tm):
            product = nn(coefs, spread[:, width * t : width * (t + 1)])
            for c in range(own):
                for b in range(chunks):
                    block = product[LANES * c : LANES * (c + 1), LANES * b : LANES * (b + 1)]
                    turned = pltpu.roll(block, 0, 1, stride=1, stride_axis=0)
                    inside = jnp.where(lanes >= rows, turned, 0.0)
                    beyond = turned - inside
                    near = carry[c]
                    far = jnp.zeros((SUB, LANES), F32)
                    for a in range(LANES // SUB):
                        near = near + inside[SUB * a : SUB * (a + 1)]
                        far = far + beyond[SUB * a : SUB * (a + 1)]
                    carry[c] = far
                    est_out[t, c : c + 1, LANES * b : LANES * (b + 1)] = jnp.sum(near, axis=0, keepdims=True)

    for off in range(1, n_tm):
        dst = lax.rem(tm + off, n_tm)
        go(copy(est_out.at[dst], est_in.at[tm], est_send.at[off], est_recv.at[off], tm=dst))
    est_in[tm] = est_out[tm]
    for off in range(1, n_tm):
        src = lax.rem(tm + n_tm - off, n_tm)
        copy(est_out.at[src], est_in.at[src], est_send.at[off], est_recv.at[off], tm=src).wait_recv()
    estimate = jnp.concatenate([est_in[i] for i in range(n_tm)], axis=0)
    position = tm * width + lax.broadcasted_iota(jnp.int32, (traces, width), 1)
    counts = jnp.minimum(position + 1, taps).astype(F32)
    out[...] = jnp.where(sampled[...] == 1, observed[...].astype(F32), estimate / counts)
    for c in pending:
        c.wait_send()


def on_device(observed, sampled, probes):
    n_tm, n_tr = lax.axis_size("tm"), lax.axis_size("trace")
    taps, traces, count = probes.shape
    width = observed.shape[1]
    groups = taps // LANES
    chunks = width // LANES
    total = n_tm * chunks
    own = traces // n_tm
    n_z = n_tm // 2
    probes = probes.reshape(groups, LANES * traces, count)
    vmem = pl.BlockSpec(memory_space=pltpu.VMEM)
    dma = pltpu.SemaphoreType.DMA
    return pl.pallas_call(
        functools.partial(kernel, n_tm, n_tr),
        out_shape=jax.ShapeDtypeStruct((traces, width), F32),
        in_specs=[vmem] * 3,
        out_specs=vmem,
        scratch_shapes=[
            pltpu.VMEM((traces, width), BF),
            pltpu.VMEM((traces, taps), BF),
            pltpu.VMEM((n_tm, own, width), F32),
            pltpu.VMEM((n_tm, own, width), F32),
            pltpu.VMEM((LANES * traces, width + taps - LANES), BF),
            pltpu.VMEM((groups * count, LANES * traces), BF),
            pltpu.VMEM((chunks * count, LANES), BF),
            pltpu.VMEM((n_tr, chunks * count // n_tr, LANES), BF),
            pltpu.VMEM((n_tm, chunks * count, LANES), BF),
            pltpu.VMEM((count, n_tm * width), BF),
            pltpu.VMEM((own * LANES, (total + groups - 1) * LANES), BF),
            pltpu.VMEM((groups * count, (total + groups - 1) * LANES), BF),
            pltpu.VMEM((n_tm, own, width), F32),
            pltpu.VMEM((n_tm, own, width), F32),
            dma((2,)),
            dma((n_tm,)), dma((n_tm,)),
            dma((n_tr,)), dma((n_tr,)),
            dma((n_z,)), dma((n_z,)),
            dma((n_z, n_tr)), dma((n_z, n_tr)),
            dma((n_z, n_tr)), dma((n_z, n_tr)),
            dma((n_tm,)), dma((n_tm,)),
        ],
        compiler_params=pltpu.CompilerParams(
            collective_id=0, has_side_effects=True, vmem_limit_bytes=56 * 1024 * 1024
        ),
        cost_estimate=pl.CostEstimate(flops=2 * 10**9, bytes_accessed=2 * 10**6, transcendentals=0),
    )(observed, sampled, probes)


def solution(mesh):
    in_specs = (P("trace", "tm"), P("trace", "tm"), P(None, "trace", None))
    out_specs = P("trace", "tm")
    return jax.shard_map(
        on_device, mesh=mesh, in_specs=in_specs, out_specs=out_specs, check_vma=False
    )
```

profile of v0, /device:TPU:0, one launch (start us, length us, event | category | flops | bytes accessed | tf_op | source)
XLA Modules:
  0.0 36.6 jit_solution(1039101353026643713)
XLA Ops:
  0.0 35.2 %shard_map.37 = f32[16,512]{1,0:T(8,128)} custom-call(bf16[16,512]{1,0:T(8,128)(2,1)} %observed.1, s32[16,512]{1,0:T(8,128)} %sampled.1, bf16[2,2048,128]{2,1,0:T(8,128)(2,1)} %bitcast.1), custom_call_target="tpu_custom_call" | custom-call | flops 2000000000 | bytes 2000000 | tf_op jit(solution)/shard_map/pallas_call | solution.py:292
  35.2 1.4 %copy.5 = f32[16,512]{1,0:T(8,128)} copy(f32[16,512]{1,0:T(8,128)} %shard_map.37) | data formatting | bytes 65536
where the time goes:
time: 36.8 us; the launch traced here: 36.6 us
  Pallas kernels  35.2 us (96%)
  local copies, waits for them, and re-layouts  1.38 us (4%)
    pallas_call x1, Pallas kernels, on_device(): pl.pallas_call(functools.partial(kernel, n_tm, n_tr), out_shape=jax.Shape...  35.2 us
    unnamed x1, local copies, waits for them, and re-layouts  1.38 us

commit v1 on v0

--- a/solution.py
+++ b/solution.py
@@ -32,40 +32,65 @@
 def inverse_factor(gram):
     size = gram.shape[0]
     blocks = size // SUB
+    full_rows = lax.broadcasted_iota(jnp.int32, (size, size), 0)
+    full_lanes = lax.broadcasted_iota(jnp.int32, (size, size), 1)
+    diagonal = jnp.where(full_rows == full_lanes, gram, 0.0)
+    by_row = lax.rsqrt(jnp.sum(diagonal, axis=1, keepdims=True))
+    by_lane = lax.rsqrt(jnp.sum(diagonal, axis=0, keepdims=True))
+    gram = gram * by_row * by_lane
     rows = lax.broadcasted_iota(jnp.int32, (SUB, size), 0)
     lanes = lax.broadcasted_iota(jnp.int32, (SUB, size), 1)
     left = [gram[SUB * a : SUB * (a + 1)] for a in range(blocks)]
     right = [jnp.where(lanes == rows + SUB * a, 1.0, 0.0).astype(F32) for a in range(blocks)]
-    scales = []
+    found = []
+
+    def at(x, s):
+        return jnp.broadcast_to(x[s : s + 1], (SUB, size))
+
     for a0 in range(blocks):
-        wide = {
+        columns = {
             a: [jnp.broadcast_to(left[a][:, SUB * a0 + q : SUB * a0 + q + 1], (SUB, size)) for q in range(SUB)]
             for a in range(a0, blocks)
         }
-        scale = jnp.zeros((SUB, size), F32)
-        for s in range(SUB):
-            pivot = wide[a0][s][s : s + 1]
-            inverse = 1.0 / pivot
-            scale = jnp.where(rows == s, pivot, scale)
-            row_left = left[a0][s : s + 1] * inverse
-            row_right = right[a0][s : s + 1] * inverse
-            row_wide = {q: wide[a0][q][s : s + 1] * inverse for q in range(s + 1, SUB)}
-            for a in range(a0, blocks):
-                factor = wide[a][s]
-                if a == a0:
-                    factor = jnp.where(rows > s, factor, 0.0)
-                left[a] = left[a] - factor * row_left
-                right[a] = right[a] - factor * row_right
-                for q in range(s + 1, SUB):
-                    wide[a][q] = wide[a][q] - factor * row_wide[q]
-        scales.append(lax.rsqrt(scale))
-    return jnp.concatenate([right[a] * scales[a] for a in range(blocks)], axis=0)
+        wide = columns.pop(a0)
+        panel = {"left": left[a0], "right": right[a0]}
+        taken = jnp.zeros((SUB, size), F32)
+        scale = jnp.ones((SUB, size), F32)
+        for s in range(0, SUB, 2):
+            first, second = wide[s], wide[s + 1]
+            p, q, r = at(first, s), at(first, s + 1), at(second, s + 1)
+            det = p * r - q * q
+            inverse = 1.0 / det
+            here = (rows == s) | (rows == s + 1)
+            f0, f1 = jnp.where(here, 0.0, first), jnp.where(here, 0.0, second)
+
+            def eliminate(x):
+                x0, x1 = at(x, s), at(x, s + 1)
+                y0 = (r * x0 - q * x1) * inverse
+                y1 = (p * x1 - q * x0) * inverse
+                rest = jnp.where(rows == s, y0, jnp.where(rows == s + 1, y1, x))
+                return rest - (f0 * y0 + f1 * y1)
+
+            x0, x1 = at(panel["right"], s), at(panel["right"], s + 1)
+            taken = jnp.where(rows == s, x0, jnp.where(rows == s + 1, x1 - (q / p) * x0, taken))
+            scale = jnp.where(rows == s, p, jnp.where(rows == s + 1, det / p, scale))
+            for k in range(s + 2, SUB):
+                wide[k] = eliminate(wide[k])
+            panel = {side: eliminate(x) for side, x in panel.items()}
+        found.append(taken * lax.rsqrt(scale))
+        solved_left = [at(panel["left"], s) for s in range(SUB)]
+        solved_right = [at(panel["right"], s) for s in range(SUB)]
+        for a in range(a0 + 1, blocks):
+            for q in range(SUB):
+                left[a] = left[a] - columns[a][q] * solved_left[q]
+                right[a] = right[a] - columns[a][q] * solved_right[q]
+    return jnp.concatenate(found, axis=0) * by_lane
 
 
 def kernel(
     n_tm, n_tr,
-    observed, sampled, probes, out,
-    data, halo, slices, windows, rolled, probes_t, part, parts_in, sketch, flat,
+    observed, sampled, probes_in, out,
+    probes, probes_sem, data, halo, slices, windows, rolled, probes_t, part, parts_in, sketch, flat,
     hankel, spread, est_out, est_in,
     halo_sems, win_send, win_recv, part_send, part_recv,
     z_send, z_recv, x_send, x_recv, c_send, c_recv, est_send, est_recv,
@@ -78,6 +103,8 @@
     traces, width = data.shape
     own = traces // n_tm
     groups, contract, probe_count = probes.shape
+    fetch = pltpu.make_async_copy(probes_in, probes, probes_sem)
+    fetch.start()
     taps = groups * LANES
     chunks = width // LANES
     total = n_tm * chunks
@@ -114,6 +141,7 @@
         pending.append(c)
     windows[tm] = slices[tm]
 
+    fetch.wait()
     with jax.named_scope("probes_transposed"):
         for g in range(groups):
             probes_t[probe_count * g : probe_count * (g + 1), :] = probes[g].T
@@ -124,10 +152,14 @@
         extended = jnp.concatenate([masked, tail], axis=1)
         reach = extended.shape[1]
         keep = rolled.shape[1]
-        for j in range(LANES):
-            moved = pltpu.roll(extended, reach - j, 1) if j else extended
-            rolled[traces * j : traces * (j + 1), :] = moved[:, :keep].astype(BF)
-        both = nn(probes_t[...], rolled[...])
+        both = jnp.zeros((groups * probe_count, keep), F32)
+        step = LANES // 4
+        for first in range(0, LANES, step):
+            for j in range(first, first + step):
+                moved = pltpu.roll(extended, reach - j, 1) if j else extended
+                rolled[traces * j : traces * (j + 1), :] = moved[:, :keep].astype(BF)
+            some = slice(traces * first, traces * (first + step))
+            both = both + nn(probes_t[:, some], rolled[some, :])
         for b in range(chunks):
             block = both[:probe_count, LANES * b : LANES * (b + 1)]
             for g in range(1, groups):
@@ -186,46 +218,52 @@
     for off in range(1, n_tm):
         src = lax.rem(tm + n_tm - off, n_tm)
         copy(slices.at[src], windows.at[src], win_send.at[off], win_recv.at[off], tm=src).wait_recv()
-    with jax.named_scope("hankel"):
-        rows = lax.broadcasted_iota(jnp.int32, (LANES, LANES), 0)
-        lanes = lax.broadcasted_iota(jnp.int32, (LANES, LANES), 1)
-        for c in range(own):
-            ahead = None
-            for m in range(total + groups - 2, -1, -1):
-                if m < total:
-                    t, b = m // chunks, m % chunks
-                    line = windows[t, c : c + 1, LANES * b : LANES * (b + 1)]
-                    now = pltpu.roll(jnp.broadcast_to(line, (LANES, LANES)), 1, 1, stride=1, stride_axis=0)
-                else:
-                    now = jnp.zeros((LANES, LANES), F32)
-                if ahead is None:
-                    ahead = jnp.zeros((LANES, LANES), F32)
-                hankel[LANES * c : LANES * (c + 1), LANES * m : LANES * (m + 1)] = jnp.where(
-                    lanes <= rows, now, ahead
-                ).astype(BF)
-                ahead = now
-
+    rows = lax.broadcasted_iota(jnp.int32, (LANES, LANES), 0)
+    lanes = lax.broadcasted_iota(jnp.int32, (LANES, LANES), 1)
+
+    @jax.named_scope("hankel")
+    def hankel_of(c):
+        ahead = jnp.zeros((LANES, LANES), F32)
+        for m in range(total + groups - 2, -1, -1):
+            if m < total:
+                t, b = m // chunks, m % chunks
+                line = windows[t, c : c + 1, LANES * b : LANES * (b + 1)]
+                now = pltpu.roll(jnp.broadcast_to(line, (LANES, LANES)), 1, 1, stride=1, stride_axis=0)
+            else:
+                now = jnp.zeros((LANES, LANES), F32)
+            hankel[LANES * c : LANES * (c + 1), LANES * m : LANES * (m + 1)] = jnp.where(
+                lanes <= rows, now, ahead
+            ).astype(BF)
+            ahead = now
+
+    @jax.named_scope("gram")
+    def gram_of(t):
+        for b in range(chunks):
+            flat[t, :, LANES * b : LANES * (b + 1)] = sketch[t, probe_count * b : probe_count * (b + 1), :]
+        return nt(flat[t], flat[t])
+
+    for c in range(own // 2):
+        hankel_of(c)
     for zo in range(1, n_z):
         arrived(zo, 0, z_send.at[zo], z_recv.at[zo], core)
         for ro in range(1, n_tr):
             go(across(zo, ro))
         go(to_sibling(zo, 0))
+    for c in range(own // 2, own):
+        hankel_of(c)
+    gram = jnp.zeros((probe_count, probe_count), F32)
     for zo in range(n_z):
         for ro in range(1, n_tr):
             arrived(zo, ro, x_send.at[zo, ro], x_recv.at[zo, ro], core)
             go(to_sibling(zo, ro))
+        gram = gram + gram_of(lax.rem(z + n_z - zo, n_z) * 2 + core)
     for zo in range(n_z):
         for ro in range(n_tr):
             arrived(zo, ro, c_send.at[zo, ro], c_recv.at[zo, ro], 1 - core)
-
-    with jax.named_scope("gram"):
-        for t in range(n_tm):
-            for b in range(chunks):
-                m = t * chunks + b
-                flat[:, LANES * m : LANES * (m + 1)] = sketch[t, probe_count * b : probe_count * (b + 1), :]
-        gram = nt(flat[...], flat[...])
+        gram = gram + gram_of(lax.rem(z + n_z - zo, n_z) * 2 + 1 - core)
+
     with jax.named_scope("inverse_factor"):
-        hi, mid, low = split3(inverse_factor(gram))
+        splits = jnp.concatenate(split3(inverse_factor(gram)), axis=0)
     with jax.named_scope("basis"):
         for g in range(groups):
             rows_g = slice(probe_count * g, probe_count * (g + 1))
@@ -234,8 +272,9 @@
             if g < groups - 1:
                 spread[rows_g, LANES * (total + g) :] = jnp.zeros((probe_count, LANES * (groups - 1 - g)), BF)
         for t in range(n_tm):
-            piece = flat[:, width * t : width * (t + 1)]
-            basis = (nn(low, piece) + nn(mid, piece) + nn(hi, piece)).astype(BF)
+            product = nn(splits, flat[t])
+            hi, mid, low = (product[probe_count * i : probe_count * (i + 1)] for i in range(3))
+            basis = (low + mid + hi).astype(BF)
             for g in range(groups):
                 spread[probe_count * g : probe_count * (g + 1), width * t + LANES * g : width * (t + 1) + LANES * g] = basis
     with jax.named_scope("coefs"):
@@ -269,10 +308,8 @@
     for off in range(1, n_tm):
         src = lax.rem(tm + n_tm - off, n_tm)
         copy(est_out.at[src], est_in.at[src], est_send.at[off], est_recv.at[off], tm=src).wait_recv()
-    estimate = jnp.concatenate([est_in[i] for i in range(n_tm)], axis=0)
-    position = tm * width + lax.broadcasted_iota(jnp.int32, (traces, width), 1)
-    counts = jnp.minimum(position + 1, taps).astype(F32)
-    out[...] = jnp.where(sampled[...] == 1, observed[...].astype(F32), estimate / counts)
+    for i in range(n_tm):
+        out[own * i : own * (i + 1), :] = est_in[i]
     for c in pending:
         c.wait_send()
 
@@ -289,12 +326,13 @@
     probes = probes.reshape(groups, LANES * traces, count)
     vmem = pl.BlockSpec(memory_space=pltpu.VMEM)
     dma = pltpu.SemaphoreType.DMA
-    return pl.pallas_call(
+    summed = pl.pallas_call(
         functools.partial(kernel, n_tm, n_tr),
         out_shape=jax.ShapeDtypeStruct((traces, width), F32),
-        in_specs=[vmem] * 3,
+        in_specs=[vmem, vmem, pl.BlockSpec(memory_space=pl.ANY)],
         out_specs=vmem,
         scratch_shapes=[
+            pltpu.VMEM(probes.shape, BF), dma,
             pltpu.VMEM((traces, width), BF),
             pltpu.VMEM((traces, taps), BF),
             pltpu.VMEM((n_tm, own, width), F32),
@@ -304,7 +342,7 @@
             pltpu.VMEM((chunks * count, LANES), BF),
             pltpu.VMEM((n_tr, chunks * count // n_tr, LANES), BF),
             pltpu.VMEM((n_tm, chunks * count, LANES), BF),
-            pltpu.VMEM((count, n_tm * width), BF),
+            pltpu.VMEM((n_tm, count, width), BF),
             pltpu.VMEM((own * LANES, (total + groups - 1) * LANES), BF),
             pltpu.VMEM((groups * count, (total + groups - 1) * LANES), BF),
             pltpu.VMEM((n_tm, own, width), F32),
@@ -322,6 +360,9 @@
         ),
         cost_estimate=pl.CostEstimate(flops=2 * 10**9, bytes_accessed=2 * 10**6, transcendentals=0),
     )(observed, sampled, probes)
+    position = lax.axis_index("tm") * width + jnp.arange(width, dtype=jnp.int32)
+    counts = jnp.minimum(position + 1, taps).astype(F32)
+    return jnp.where(sampled == 1, observed.astype(F32), summed / counts[None, :])
 
 
 def solution(mesh):

time: 36.8 us -> 36.2 us (0.984)
  other arithmetic: 0 us -> 1.39 us
  local copies, waits for them, and re-layouts: 1.38 us -> 0.01 us
  Pallas kernels: 35.2 us -> 34.5 us
    select_n x0 -> x1, other arithmetic: none -> 1.38 us  [on_device(): jnp.where(sampled == 1, observed.astype(F32), summed / counts[None, :])]
    unnamed x1 -> x4, local copies, waits for them, and re-layouts: 1.38 us -> 0.01 us
    pallas_call x1, Pallas kernels: 35.2 us -> 34.5 us  [on_device(): pl.pallas_call(functools.partial(kernel, n_tm, n_tr), out_shape=jax.Shape...]
where the time goes in v1:
time: 36.2 us; the launch traced here: 35.9 us
  Pallas kernels  34.5 us (95%)
  other arithmetic  1.39 us (4%)
    pallas_call x1, Pallas kernels, on_device(): pl.pallas_call(functools.partial(kernel, n_tm, n_tr), out_shape=jax.Shape...  34.5 us
    select_n x1, other arithmetic, on_device(): jnp.where(sampled == 1, observed.astype(F32), summed / counts[None, :])  1.38 us

profile of v1, /device:TPU:0, one launch (start us, length us, event | category | flops | bytes accessed | tf_op | source)
XLA Modules:
  0.0 35.9 jit_solution(1105436613247534239)
XLA Ops:
  0.0 0.0 copy-start
  0.0 0.0 copy-start.1
  0.0 34.5 %shard_map.37 = f32[16,512]{1,0:T(8,128)} custom-call(bf16[16,512]{1,0:T(8,128)(2,1)} %observed.1, s32[16,512]{1,0:T(8,128)} %sampled.1, bf16[2,2048,128]{2,1,0:T(8,128)(2,1)} %bitcast.1), custom_call_target="tpu_custom_call" | custom-call | flops 2000000000 | bytes 2000000 | tf_op jit(solution)/shard_map/pallas_call | solution.py:329
  34.5 0.0 copy-done
  34.5 0.0 copy-done.1
  34.5 1.4 %divide_select_fusion = f32[16,512]{1,0:T(8,128)} fusion(f32[16,512]{1,0:T(8,128)} %shard_map.37, bf16[16,512]{1,0:T(8,128)(2,1)S(1)} %copy-done.1, s32[16,512]{1,0:T(8,128)S(1)} %copy-done, f32[512]{0:T(512)S(1)} %minimum_convert_fusion), kind=kLoop, calls=%fused_computation | loop fusion | flops 32768 | bytes 116736 | tf_op jit(solution)/shard_map/jit(_where)/select_n | solution.py:365
  (1 shorter events, 0.0 us)
Async XLA Ops:
  0.0 34.5 %copy-start = (s32[16,512]{1,0:T(8,128)S(1)}, s32[16,512]{1,0:T(8,128)}, u32[]{:S(2)}) copy-start(s32[16,512]{1,0:T(8,128)} %sampled.1) | copy-start | bytes 98308
  0.0 34.5 %copy-start.1 = (bf16[16,512]{1,0:T(8,128)(2,1)S(1)}, bf16[16,512]{1,0:T(8,128)(2,1)}, u32[]{:S(2)}) copy-start(bf16[16,512]{1,0:T(8,128)(2,1)} %observed.1) | copy-start | bytes 49156

commit v2 on v1

--- a/solution.py
+++ b/solution.py
@@ -29,69 +29,78 @@
     return hi, mid, low
 
 
-def inverse_factor(gram):
+def panel_step(step, size, below, left, right, found):
+    rows = lax.broadcasted_iota(jnp.int32, (SUB, size), 0)
+
+    def at(x, s):
+        return jnp.broadcast_to(x[s : s + 1], (SUB, size))
+
+    panel = [left[0:SUB, :], right[0:SUB, :]]
+    wide = [jnp.broadcast_to(panel[0][:, q : q + 1], (SUB, size)) for q in range(SUB)]
+    taken = jnp.zeros((SUB, size), F32)
+    scale = jnp.ones((SUB, size), F32)
+    for s in range(0, SUB, 2):
+        first, second = wide[s], wide[s + 1]
+        p, q, r = at(first, s), at(first, s + 1), at(second, s + 1)
+        det = p * r - q * q
+        inverse = 1.0 / det
+        here = (rows == s) | (rows == s + 1)
+        f0, f1 = jnp.where(here, 0.0, first), jnp.where(here, 0.0, second)
+
+        def eliminate(x):
+            x0, x1 = at(x, s), at(x, s + 1)
+            y0 = (r * x0 - q * x1) * inverse
+            y1 = (p * x1 - q * x0) * inverse
+            rest = jnp.where(rows == s, y0, jnp.where(rows == s + 1, y1, x))
+            return rest - (f0 * y0 + f1 * y1)
+
+        x0, x1 = at(panel[1], s), at(panel[1], s + 1)
+        taken = jnp.where(rows == s, x0, jnp.where(rows == s + 1, x1 - (q / p) * x0, taken))
+        scale = jnp.where(rows == s, p, jnp.where(rows == s + 1, det / p, scale))
+        for k in range(s + 2, SUB):
+            wide[k] = eliminate(wide[k])
+        panel = [eliminate(x) for x in panel]
+    found[pl.ds(pl.multiple_of(step * SUB, SUB), SUB), :] = taken * lax.rsqrt(scale)
+    solved = [[at(x, s) for s in range(SUB)] for x in panel]
+    for a in range(1, below + 1):
+        here, up = slice(SUB * a, SUB * (a + 1)), slice(SUB * (a - 1), SUB * a)
+        x, y = left[here, :], right[here, :]
+        factors = [jnp.broadcast_to(x[:, q : q + 1], (SUB, size)) for q in range(SUB)]
+        for q in range(SUB):
+            x = x - factors[q] * solved[0][q]
+            y = y - factors[q] * solved[1][q]
+        left[up, :] = pltpu.roll(x, size - SUB, 1)
+        right[up, :] = y
+
+
+def inverse_factor(gram, left, right, found):
     size = gram.shape[0]
-    blocks = size // SUB
-    full_rows = lax.broadcasted_iota(jnp.int32, (size, size), 0)
-    full_lanes = lax.broadcasted_iota(jnp.int32, (size, size), 1)
-    diagonal = jnp.where(full_rows == full_lanes, gram, 0.0)
+    rows = lax.broadcasted_iota(jnp.int32, (size, size), 0)
+    lanes = lax.broadcasted_iota(jnp.int32, (size, size), 1)
+    diagonal = jnp.where(rows == lanes, gram, 0.0)
     by_row = lax.rsqrt(jnp.sum(diagonal, axis=1, keepdims=True))
     by_lane = lax.rsqrt(jnp.sum(diagonal, axis=0, keepdims=True))
-    gram = gram * by_row * by_lane
-    rows = lax.broadcasted_iota(jnp.int32, (SUB, size), 0)
-    lanes = lax.broadcasted_iota(jnp.int32, (SUB, size), 1)
-    left = [gram[SUB * a : SUB * (a + 1)] for a in range(blocks)]
-    right = [jnp.where(lanes == rows + SUB * a, 1.0, 0.0).astype(F32) for a in range(blocks)]
-    found = []
-
-    def at(x, s):
-        return jnp.broadcast_to(x[s : s + 1], (SUB, size))
-
-    for a0 in range(blocks):
-        columns = {
-            a: [jnp.broadcast_to(left[a][:, SUB * a0 + q : SUB * a0 + q + 1], (SUB, size)) for q in range(SUB)]
-            for a in range(a0, blocks)
-        }
-        wide = columns.pop(a0)
-        panel = {"left": left[a0], "right": right[a0]}
-        taken = jnp.zeros((SUB, size), F32)
-        scale = jnp.ones((SUB, size), F32)
-        for s in range(0, SUB, 2):
-            first, second = wide[s], wide[s + 1]
-            p, q, r = at(first, s), at(first, s + 1), at(second, s + 1)
-            det = p * r - q * q
-            inverse = 1.0 / det
-            here = (rows == s) | (rows == s + 1)
-            f0, f1 = jnp.where(here, 0.0, first), jnp.where(here, 0.0, second)
-
-            def eliminate(x):
-                x0, x1 = at(x, s), at(x, s + 1)
-                y0 = (r * x0 - q * x1) * inverse
-                y1 = (p * x1 - q * x0) * inverse
-                rest = jnp.where(rows == s, y0, jnp.where(rows == s + 1, y1, x))
-                return rest - (f0 * y0 + f1 * y1)
-
-            x0, x1 = at(panel["right"], s), at(panel["right"], s + 1)
-            taken = jnp.where(rows == s, x0, jnp.where(rows == s + 1, x1 - (q / p) * x0, taken))
-            scale = jnp.where(rows == s, p, jnp.where(rows == s + 1, det / p, scale))
-            for k in range(s + 2, SUB):
-                wide[k] = eliminate(wide[k])
-            panel = {side: eliminate(x) for side, x in panel.items()}
-        found.append(taken * lax.rsqrt(scale))
-        solved_left = [at(panel["left"], s) for s in range(SUB)]
-        solved_right = [at(panel["right"], s) for s in range(SUB)]
-        for a in range(a0 + 1, blocks):
-            for q in range(SUB):
-                left[a] = left[a] - columns[a][q] * solved_left[q]
-                right[a] = right[a] - columns[a][q] * solved_right[q]
-    return jnp.concatenate(found, axis=0) * by_lane
+    left[...] = gram * by_row * by_lane
+    right[...] = jnp.where(rows == lanes, 1.0, 0.0).astype(F32)
+    blocks = size // SUB
+    half = blocks // 2
+
+    @pl.loop(0, half)
+    def _(step):
+        panel_step(step, size, blocks - 1, left, right, found)
+
+    @pl.loop(half, blocks)
+    def _(step):
+        panel_step(step, size, blocks - half - 1, left, right, found)
+
+    return found[...] * by_lane
 
 
 def kernel(
     n_tm, n_tr,
     observed, sampled, probes_in, out,
     probes, probes_sem, data, halo, slices, windows, rolled, probes_t, part, parts_in, sketch, flat,
-    hankel, spread, est_out, est_in,
+    hankel, spread, est_out, est_in, left, right, found, total_coefs,
     halo_sems, win_send, win_recv, part_send, part_recv,
     z_send, z_recv, x_send, x_recv, c_send, c_recv, est_send, est_recv,
 ):
@@ -143,23 +152,27 @@
 
     fetch.wait()
     with jax.named_scope("probes_transposed"):
-        for g in range(groups):
-            probes_t[probe_count * g : probe_count * (g + 1), :] = probes[g].T
+        @pl.loop(0, contract // LANES, unroll=2)
+        def _(i):
+            some = pl.ds(pl.multiple_of(i * LANES, LANES), LANES)
+            for g in range(groups):
+                probes_t[probe_count * g : probe_count * (g + 1), some] = probes[g, some, :].T
 
     halo_copy.wait_recv()
     with jax.named_scope("sketch_part"):
         tail = jnp.where(tm < n_tm - 1, halo[...].astype(F32), 0.0)
         extended = jnp.concatenate([masked, tail], axis=1)
-        reach = extended.shape[1]
         keep = rolled.shape[1]
-        both = jnp.zeros((groups * probe_count, keep), F32)
-        step = LANES // 4
-        for first in range(0, LANES, step):
-            for j in range(first, first + step):
-                moved = pltpu.roll(extended, reach - j, 1) if j else extended
-                rolled[traces * j : traces * (j + 1), :] = moved[:, :keep].astype(BF)
-            some = slice(traces * first, traces * (first + step))
-            both = both + nn(probes_t[:, some], rolled[some, :])
+        lane = lax.broadcasted_iota(jnp.int32, (traces, LANES), 1)
+        parts = [extended[:, LANES * m : LANES * (m + 1)] for m in range(keep // LANES + 1)]
+
+        @pl.loop(0, LANES, unroll=8)
+        def _(j):
+            turned = [pltpu.roll(x, lax.rem(LANES - j, LANES), 1) for x in parts]
+            moved = [jnp.where(lane < LANES - j, x, y).astype(BF) for x, y in zip(turned, turned[1:])]
+            rolled[pl.ds(pl.multiple_of(j * traces, traces), traces), :] = jnp.concatenate(moved, axis=1)
+
+        both = nn(probes_t[...], rolled[...])
         for b in range(chunks):
             block = both[:probe_count, LANES * b : LANES * (b + 1)]
             for g in range(1, groups):
@@ -221,20 +234,25 @@
     rows = lax.broadcasted_iota(jnp.int32, (LANES, LANES), 0)
     lanes = lax.broadcasted_iota(jnp.int32, (LANES, LANES), 1)
 
+    for k in range(groups - 1):
+        hankel[:, LANES * (total + k) :] = jnp.zeros((own * LANES, LANES * (groups - 1 - k)), BF)
+
     @jax.named_scope("hankel")
     def hankel_of(c):
-        ahead = jnp.zeros((LANES, LANES), F32)
-        for m in range(total + groups - 2, -1, -1):
-            if m < total:
-                t, b = m // chunks, m % chunks
-                line = windows[t, c : c + 1, LANES * b : LANES * (b + 1)]
-                now = pltpu.roll(jnp.broadcast_to(line, (LANES, LANES)), 1, 1, stride=1, stride_axis=0)
-            else:
-                now = jnp.zeros((LANES, LANES), F32)
-            hankel[LANES * c : LANES * (c + 1), LANES * m : LANES * (m + 1)] = jnp.where(
-                lanes <= rows, now, ahead
-            ).astype(BF)
-            ahead = now
+        def turned(t, b):
+            line = windows[t, c : c + 1, LANES * b : LANES * (b + 1)]
+            return pltpu.roll(jnp.broadcast_to(line, (LANES, LANES)), 1, 1, stride=1, stride_axis=0)
+
+        def some(i, ahead):
+            t = n_tm - 1 - i
+            for b in range(chunks - 1, -1, -1):
+                now = turned(t, b)
+                to = pl.ds(pl.multiple_of(t * width + LANES * b, LANES), LANES)
+                hankel[LANES * c : LANES * (c + 1), to] = jnp.where(lanes <= rows, now, ahead).astype(BF)
+                ahead = now
+            return ahead
+
+        lax.fori_loop(0, n_tm, some, jnp.zeros((LANES, LANES), F32))
 
     @jax.named_scope("gram")
     def gram_of(t):
@@ -251,19 +269,22 @@
         go(to_sibling(zo, 0))
     for c in range(own // 2, own):
         hankel_of(c)
-    gram = jnp.zeros((probe_count, probe_count), F32)
-    for zo in range(n_z):
+    def from_across(zo, gram):
         for ro in range(1, n_tr):
             arrived(zo, ro, x_send.at[zo, ro], x_recv.at[zo, ro], core)
-            go(to_sibling(zo, ro))
-        gram = gram + gram_of(lax.rem(z + n_z - zo, n_z) * 2 + core)
-    for zo in range(n_z):
+            to_sibling(zo, ro).start()
+        return gram + gram_of(lax.rem(z + n_z - zo, n_z) * 2 + core)
+
+    def from_sibling(zo, gram):
         for ro in range(n_tr):
             arrived(zo, ro, c_send.at[zo, ro], c_recv.at[zo, ro], 1 - core)
-        gram = gram + gram_of(lax.rem(z + n_z - zo, n_z) * 2 + 1 - core)
+        return gram + gram_of(lax.rem(z + n_z - zo, n_z) * 2 + 1 - core)
+
+    gram = lax.fori_loop(0, n_z, from_across, jnp.zeros((probe_count, probe_count), F32))
+    gram = lax.fori_loop(0, n_z, from_sibling, gram)
 
     with jax.named_scope("inverse_factor"):
-        splits = jnp.concatenate(split3(inverse_factor(gram)), axis=0)
+        splits = jnp.concatenate(split3(inverse_factor(gram, left, right, found)), axis=0)
     with jax.named_scope("basis"):
         for g in range(groups):
             rows_g = slice(probe_count * g, probe_count * (g + 1))
@@ -271,22 +292,32 @@
                 spread[rows_g, : LANES * g] = jnp.zeros((probe_count, LANES * g), BF)
             if g < groups - 1:
                 spread[rows_g, LANES * (total + g) :] = jnp.zeros((probe_count, LANES * (groups - 1 - g)), BF)
-        for t in range(n_tm):
+
+        @pl.loop(0, n_tm)
+        def _(t):
             product = nn(splits, flat[t])
             hi, mid, low = (product[probe_count * i : probe_count * (i + 1)] for i in range(3))
             basis = (low + mid + hi).astype(BF)
             for g in range(groups):
-                spread[probe_count * g : probe_count * (g + 1), width * t + LANES * g : width * (t + 1) + LANES * g] = basis
+                to = pl.ds(pl.multiple_of(t * width + LANES * g, LANES), width)
+                spread[probe_count * g : probe_count * (g + 1), to] = basis
     with jax.named_scope("coefs"):
-        coefs = nt(hankel[...], spread[...]).astype(BF)
+        total_coefs[...] = nt(hankel[:, LANES * total :], spread[:, LANES * total :])
+
+        @pl.loop(0, n_tm // 2)
+        def _(i):
+            some = pl.ds(pl.multiple_of(i * 2 * width, LANES), 2 * width)
+            total_coefs[...] += nt(hankel[:, some], spread[:, some])
+
+        coefs = total_coefs[...].astype(BF)
         flip = jnp.where(lanes + rows == LANES - 1, 1.0, 0.0).astype(BF)
         coefs = jnp.concatenate(
             [nn(flip, coefs[LANES * c : LANES * (c + 1)]).astype(BF) for c in range(own)], axis=0
         )
     with jax.named_scope("antidiagonals"):
-        carry = [jnp.zeros((SUB, LANES), F32) for _ in range(own)]
-        for t in range(n_tm):
-            product = nn(coefs, spread[:, width * t : width * (t + 1)])
+        def some_sums(t, carry):
+            carry = list(carry)
+            product = nn(coefs, spread[:, pl.ds(pl.multiple_of(t * width, LANES), width)])
             for c in range(own):
                 for b in range(chunks):
                     block = product[LANES * c : LANES * (c + 1), LANES * b : LANES * (b + 1)]
@@ -300,6 +331,9 @@
                         far = far + beyond[SUB * a : SUB * (a + 1)]
                     carry[c] = far
                     est_out[t, c : c + 1, LANES * b : LANES * (b + 1)] = jnp.sum(near, axis=0, keepdims=True)
+            return tuple(carry)
+
+        lax.fori_loop(0, n_tm, some_sums, tuple(jnp.zeros((SUB, LANES), F32) for _ in range(own)))
 
     for off in range(1, n_tm):
         dst = lax.rem(tm + off, n_tm)
@@ -310,6 +344,11 @@
         copy(est_out.at[src], est_in.at[src], est_send.at[off], est_recv.at[off], tm=src).wait_recv()
     for i in range(n_tm):
         out[own * i : own * (i + 1), :] = est_in[i]
+    @pl.loop(0, n_z)
+    def _(zo):
+        for ro in range(1, n_tr):
+            to_sibling(zo, ro).wait_send()
+
     for c in pending:
         c.wait_send()
 
@@ -347,6 +386,10 @@
             pltpu.VMEM((groups * count, (total + groups - 1) * LANES), BF),
             pltpu.VMEM((n_tm, own, width), F32),
             pltpu.VMEM((n_tm, own, width), F32),
+            pltpu.VMEM((count, count), F32),
+            pltpu.VMEM((count, count), F32),
+            pltpu.VMEM((count, count), F32),
+            pltpu.VMEM((own * LANES, groups * count), F32),
             dma((2,)),
             dma((n_tm,)), dma((n_tm,)),
             dma((n_tr,)), dma((n_tr,)),

time: 36.2 us -> 43.5 us (1.20)
  Pallas kernels: 34.5 us -> 41.9 us
    pallas_call x1, Pallas kernels: 34.5 us -> 41.9 us  [on_device(): pl.pallas_call(functools.partial(kernel, n_tm, n_tr), out_shape=jax.Shape...]
where the time goes in v2:
time: 43.5 us; the launch traced here: 43.3 us
  Pallas kernels  41.9 us (96%)
  other arithmetic  1.39 us (3%)
    pallas_call x1, Pallas kernels, on_device(): pl.pallas_call(functools.partial(kernel, n_tm, n_tr), out_shape=jax.Shape...  41.9 us
    select_n x1, other arithmetic, on_device(): jnp.where(sampled == 1, observed.astype(F32), summed / counts[None, :])  1.38 us

profile of v2, /device:TPU:0, one launch (start us, length us, event | category | flops | bytes accessed | tf_op | source)
XLA Modules:
  0.0 43.3 jit_solution(16027275025558276573)
XLA Ops:
  0.0 0.0 copy-start
  0.0 0.0 copy-start.1
  0.0 41.9 %shard_map.37 = f32[16,512]{1,0:T(8,128)} custom-call(bf16[16,512]{1,0:T(8,128)(2,1)} %observed.1, s32[16,512]{1,0:T(8,128)} %sampled.1, bf16[2,2048,128]{2,1,0:T(8,128)(2,1)} %bitcast.1), custom_call_target="tpu_custom_call" | custom-call | flops 2000000000 | bytes 2000000 | tf_op jit(solution)/shard_map/pallas_call | solution.py:368
  41.9 0.0 copy-done
  41.9 0.0 copy-done.1
  41.9 1.4 %divide_select_fusion = f32[16,512]{1,0:T(8,128)} fusion(f32[16,512]{1,0:T(8,128)} %shard_map.37, bf16[16,512]{1,0:T(8,128)(2,1)S(1)} %copy-done.1, s32[16,512]{1,0:T(8,128)S(1)} %copy-done, f32[512]{0:T(512)S(1)} %minimum_convert_fusion), kind=kLoop, calls=%fused_computation | loop fusion | flops 32768 | bytes 116736 | tf_op jit(solution)/shard_map/jit(_where)/select_n | solution.py:408
  (1 shorter events, 0.0 us)
Async XLA Ops:
  0.0 41.9 %copy-start = (s32[16,512]{1,0:T(8,128)S(1)}, s32[16,512]{1,0:T(8,128)}, u32[]{:S(2)}) copy-start(s32[16,512]{1,0:T(8,128)} %sampled.1) | copy-start | bytes 98308
  0.0 41.9 %copy-start.1 = (bf16[16,512]{1,0:T(8,128)(2,1)S(1)}, bf16[16,512]{1,0:T(8,128)(2,1)}, u32[]{:S(2)}) copy-start(bf16[16,512]{1,0:T(8,128)(2,1)} %observed.1) | copy-start | bytes 49156

commit v3 on v1

--- a/solution.py
+++ b/solution.py
@@ -13,8 +13,8 @@
 F32 = jnp.float32
 
 
-def nt(a, b):
-    return lax.dot_general(a, b, (((1,), (1,)), ((), ())), preferred_element_type=F32)
+def nt(a, b, precision=None):
+    return lax.dot_general(a, b, (((1,), (1,)), ((), ())), precision=precision, preferred_element_type=F32)
 
 
 def nn(a, b):
@@ -91,7 +91,7 @@
     n_tm, n_tr,
     observed, sampled, probes_in, out,
     probes, probes_sem, data, halo, slices, windows, rolled, probes_t, part, parts_in, sketch, flat,
-    hankel, spread, est_out, est_in,
+    hankel, spread, projected, est_out, est_in,
     halo_sems, win_send, win_recv, part_send, part_recv,
     z_send, z_recv, x_send, x_recv, c_send, c_recv, est_send, est_recv,
 ):
@@ -240,6 +240,9 @@
     def gram_of(t):
         for b in range(chunks):
             flat[t, :, LANES * b : LANES * (b + 1)] = sketch[t, probe_count * b : probe_count * (b + 1), :]
+        for g in range(groups):
+            some = pl.ds(pl.multiple_of(t * width + LANES * g, LANES), width)
+            projected[g] += nt(hankel[:, some], flat[t])
         return nt(flat[t], flat[t])
 
     for c in range(own // 2):
@@ -251,6 +254,7 @@
         go(to_sibling(zo, 0))
     for c in range(own // 2, own):
         hankel_of(c)
+    projected[...] = jnp.zeros(projected.shape, F32)
     gram = jnp.zeros((probe_count, probe_count), F32)
     for zo in range(n_z):
         for ro in range(1, n_tr):
@@ -263,14 +267,13 @@
         gram = gram + gram_of(lax.rem(z + n_z - zo, n_z) * 2 + 1 - core)
 
     with jax.named_scope("inverse_factor"):
-        splits = jnp.concatenate(split3(inverse_factor(gram)), axis=0)
+        inverse = inverse_factor(gram)
+        splits = jnp.concatenate(split3(inverse), axis=0)
     with jax.named_scope("basis"):
         for g in range(groups):
             rows_g = slice(probe_count * g, probe_count * (g + 1))
             if g:
                 spread[rows_g, : LANES * g] = jnp.zeros((probe_count, LANES * g), BF)
-            if g < groups - 1:
-                spread[rows_g, LANES * (total + g) :] = jnp.zeros((probe_count, LANES * (groups - 1 - g)), BF)
         for t in range(n_tm):
             product = nn(splits, flat[t])
             hi, mid, low = (product[probe_count * i : probe_count * (i + 1)] for i in range(3))
@@ -278,7 +281,7 @@
             for g in range(groups):
                 spread[probe_count * g : probe_count * (g + 1), width * t + LANES * g : width * (t + 1) + LANES * g] = basis
     with jax.named_scope("coefs"):
-        coefs = nt(hankel[...], spread[...]).astype(BF)
+        coefs = jnp.concatenate([nt(projected[g], inverse, lax.Precision.HIGHEST) for g in range(groups)], axis=1).astype(BF)
         flip = jnp.where(lanes + rows == LANES - 1, 1.0, 0.0).astype(BF)
         coefs = jnp.concatenate(
             [nn(flip, coefs[LANES * c : LANES * (c + 1)]).astype(BF) for c in range(own)], axis=0
@@ -328,7 +331,7 @@
     dma = pltpu.SemaphoreType.DMA
     summed = pl.pallas_call(
         functools.partial(kernel, n_tm, n_tr),
-        out_shape=jax.ShapeDtypeStruct((traces, width), F32),
+        out_shape=pltpu.VMEM((traces, width), F32),
         in_specs=[vmem, vmem, pl.BlockSpec(memory_space=pl.ANY)],
         out_specs=vmem,
         scratch_shapes=[
@@ -345,6 +348,7 @@
             pltpu.VMEM((n_tm, count, width), BF),
             pltpu.VMEM((own * LANES, (total + groups - 1) * LANES), BF),
             pltpu.VMEM((groups * count, (total + groups - 1) * LANES), BF),
+            pltpu.VMEM((groups, own * LANES, count), F32),
             pltpu.VMEM((n_tm, own, width), F32),
             pltpu.VMEM((n_tm, own, width), F32),
             dma((2,)),

time: 36.2 us -> 35 us (0.967)
  other arithmetic: 1.39 us -> 0.63 us
    select_n x1, other arithmetic: 1.38 us -> 0.63 us  [on_device(): jnp.where(sampled == 1, observed.astype(F32), summed / counts[None, :])]
where the time goes in v3:
time: 35 us; the launch traced here: 34.8 us
  Pallas kernels  34.2 us (98%)
  other arithmetic  0.63 us (2%)
    pallas_call x1, Pallas kernels, on_device(): pl.pallas_call(functools.partial(kernel, n_tm, n_tr), out_shape=pltpu.VME...  34.2 us

profile of v3, /device:TPU:0, one launch (start us, length us, event | category | flops | bytes accessed | tf_op | source)
XLA Modules:
  0.0 34.8 jit_solution(6127725360385526339)
XLA Ops:
  0.0 0.0 copy-start
  0.0 0.0 copy-start.1
  0.0 34.2 %shard_map.37 = f32[16,512]{1,0:T(8,128)S(1)} custom-call(bf16[16,512]{1,0:T(8,128)(2,1)} %observed.1, s32[16,512]{1,0:T(8,128)} %sampled.1, bf16[2,2048,128]{2,1,0:T(8,128)(2,1)} %bitcast.1), custom_call_target="tpu_custom_call" | custom-call | flops 2000000000 | bytes 2000000 | tf_op jit(solution)/shard_map/pallas_call | solution.py:332
  34.2 0.0 copy-done
  34.2 0.0 copy-done.1
  34.2 0.6 %divide_select_fusion = f32[16,512]{1,0:T(8,128)} fusion(f32[16,512]{1,0:T(8,128)S(1)} %shard_map.37, bf16[16,512]{1,0:T(8,128)(2,1)S(1)} %copy-done.1, s32[16,512]{1,0:T(8,128)S(1)} %copy-done, f32[512]{0:T(512)S(1)} %minimum_convert_fusion), kind=kLoop, calls=%fused_computation | loop fusion | flops 32768 | bytes 116736 | tf_op jit(solution)/shard_map/jit(_where)/select_n | solution.py:369
  (1 shorter events, 0.0 us)
Async XLA Ops:
  0.0 34.2 %copy-start = (s32[16,512]{1,0:T(8,128)S(1)}, s32[16,512]{1,0:T(8,128)}, u32[]{:S(2)}) copy-start(s32[16,512]{1,0:T(8,128)} %sampled.1) | copy-start | bytes 98308
  0.0 34.2 %copy-start.1 = (bf16[16,512]{1,0:T(8,128)(2,1)S(1)}, bf16[16,512]{1,0:T(8,128)(2,1)}, u32[]{:S(2)}) copy-start(bf16[16,512]{1,0:T(8,128)(2,1)} %observed.1) | copy-start | bytes 49156

commit v4 on v3

--- a/solution.py
+++ b/solution.py
@@ -91,7 +91,7 @@
     n_tm, n_tr,
     observed, sampled, probes_in, out,
     probes, probes_sem, data, halo, slices, windows, rolled, probes_t, part, parts_in, sketch, flat,
-    hankel, spread, projected, est_out, est_in,
+    hankel, spread, products, est_out, est_in,
     halo_sems, win_send, win_recv, part_send, part_recv,
     z_send, z_recv, x_send, x_recv, c_send, c_recv, est_send, est_recv,
 ):
@@ -127,6 +127,10 @@
     data[...] = masked.astype(BF)
     for i in range(n_tm):
         slices[i] = masked[own * i : own * (i + 1)]
+    fetch.wait()
+    with jax.named_scope("probes_transposed"):
+        for g in range(groups):
+            probes_t[probe_count * g : probe_count * (g + 1), :] = probes[g].T
     pl.semaphore_wait(barrier, n_tm + n_tr - 2)
 
     pending = []
@@ -141,32 +145,36 @@
         pending.append(c)
     windows[tm] = slices[tm]
 
-    fetch.wait()
-    with jax.named_scope("probes_transposed"):
-        for g in range(groups):
-            probes_t[probe_count * g : probe_count * (g + 1), :] = probes[g].T
-
-    halo_copy.wait_recv()
-    with jax.named_scope("sketch_part"):
-        tail = jnp.where(tm < n_tm - 1, halo[...].astype(F32), 0.0)
-        extended = jnp.concatenate([masked, tail], axis=1)
-        reach = extended.shape[1]
-        keep = rolled.shape[1]
-        both = jnp.zeros((groups * probe_count, keep), F32)
+    def shifted(extended, to):
+        reach, keep = extended.shape[1], extended.shape[1] - LANES
+        result = jnp.zeros((groups * probe_count, keep), F32)
         step = LANES // 4
         for first in range(0, LANES, step):
             for j in range(first, first + step):
                 moved = pltpu.roll(extended, reach - j, 1) if j else extended
-                rolled[traces * j : traces * (j + 1), :] = moved[:, :keep].astype(BF)
+                rolled[traces * j : traces * (j + 1), to : to + keep] = moved[:, :keep].astype(BF)
             some = slice(traces * first, traces * (first + step))
-            both = both + nn(probes_t[:, some], rolled[some, :])
+            result = result + nn(probes_t[:, some], rolled[some, to : to + keep])
+        return result
+
+    nothing = jnp.zeros((traces, LANES), F32)
+    with jax.named_scope("sketch_part"):
+        inner = shifted(jnp.concatenate([masked, nothing], axis=1), 0)
+    halo_copy.wait_recv()
+    with jax.named_scope("sketch_part"):
+        tail = jnp.where(tm < n_tm - 1, halo[...].astype(F32), 0.0)
+        outer = shifted(jnp.concatenate([nothing, tail], axis=1), width)
         for b in range(chunks):
-            block = both[:probe_count, LANES * b : LANES * (b + 1)]
-            for g in range(1, groups):
-                block = block + both[probe_count * g : probe_count * (g + 1), LANES * (b + g) : LANES * (b + g + 1)]
+            block = jnp.zeros((probe_count, LANES), F32)
+            for g in range(groups):
+                mine = slice(probe_count * g, probe_count * (g + 1))
+                m, h = b + g, b + g - (chunks - 1)
+                if m < chunks:
+                    block = block + inner[mine, LANES * m : LANES * (m + 1)]
+                if h >= 0:
+                    block = block + outer[mine, LANES * h : LANES * (h + 1)]
             part[probe_count * b : probe_count * (b + 1), :] = block.astype(BF)
 
-    part_copies = []
     for off in range(1, n_tr):
         dst = lax.rem(tr + off, n_tr)
         c = copy(
@@ -240,10 +248,9 @@
     def gram_of(t):
         for b in range(chunks):
             flat[t, :, LANES * b : LANES * (b + 1)] = sketch[t, probe_count * b : probe_count * (b + 1), :]
-        for g in range(groups):
-            some = pl.ds(pl.multiple_of(t * width + LANES * g, LANES), width)
-            projected[g] += nt(hankel[:, some], flat[t])
-        return nt(flat[t], flat[t])
+        starts = [pl.multiple_of(t * width + LANES * g, LANES) for g in range(groups)]
+        stack = [hankel[:, pl.ds(start, width)] for start in starts] + [flat[t]]
+        products[...] += nt(jnp.concatenate(stack, axis=0), flat[t])
 
     for c in range(own // 2):
         hankel_of(c)
@@ -254,20 +261,19 @@
         go(to_sibling(zo, 0))
     for c in range(own // 2, own):
         hankel_of(c)
-    projected[...] = jnp.zeros(projected.shape, F32)
-    gram = jnp.zeros((probe_count, probe_count), F32)
+    products[...] = jnp.zeros(products.shape, F32)
     for zo in range(n_z):
         for ro in range(1, n_tr):
             arrived(zo, ro, x_send.at[zo, ro], x_recv.at[zo, ro], core)
             go(to_sibling(zo, ro))
-        gram = gram + gram_of(lax.rem(z + n_z - zo, n_z) * 2 + core)
+        gram_of(lax.rem(z + n_z - zo, n_z) * 2 + core)
     for zo in range(n_z):
         for ro in range(n_tr):
             arrived(zo, ro, c_send.at[zo, ro], c_recv.at[zo, ro], 1 - core)
-        gram = gram + gram_of(lax.rem(z + n_z - zo, n_z) * 2 + 1 - core)
+        gram_of(lax.rem(z + n_z - zo, n_z) * 2 + 1 - core)
 
     with jax.named_scope("inverse_factor"):
-        inverse = inverse_factor(gram)
+        inverse = inverse_factor(products[own * groups * LANES :, :])
         splits = jnp.concatenate(split3(inverse), axis=0)
     with jax.named_scope("basis"):
         for g in range(groups):
@@ -281,7 +287,7 @@
             for g in range(groups):
                 spread[probe_count * g : probe_count * (g + 1), width * t + LANES * g : width * (t + 1) + LANES * g] = basis
     with jax.named_scope("coefs"):
-        coefs = jnp.concatenate([nt(projected[g], inverse, lax.Precision.HIGHEST) for g in range(groups)], axis=1).astype(BF)
+        coefs = jnp.concatenate([nt(products[own * LANES * g : own * LANES * (g + 1), :], inverse, lax.Precision.HIGHEST) for g in range(groups)], axis=1).astype(BF)
         flip = jnp.where(lanes + rows == LANES - 1, 1.0, 0.0).astype(BF)
         coefs = jnp.concatenate(
             [nn(flip, coefs[LANES * c : LANES * (c + 1)]).astype(BF) for c in range(own)], axis=0
@@ -340,7 +346,7 @@
             pltpu.VMEM((traces, taps), BF),
             pltpu.VMEM((n_tm, own, width), F32),
             pltpu.VMEM((n_tm, own, width), F32),
-            pltpu.VMEM((LANES * traces, width + taps - LANES), BF),
+            pltpu.VMEM((LANES * traces, width + taps), BF),
             pltpu.VMEM((groups * count, LANES * traces), BF),
             pltpu.VMEM((chunks * count, LANES), BF),
             pltpu.VMEM((n_tr, chunks * count // n_tr, LANES), BF),
@@ -348,7 +354,7 @@
             pltpu.VMEM((n_tm, count, width), BF),
             pltpu.VMEM((own * LANES, (total + groups - 1) * LANES), BF),
             pltpu.VMEM((groups * count, (total + groups - 1) * LANES), BF),
-            pltpu.VMEM((groups, own * LANES, count), F32),
+            pltpu.VMEM((own * groups * LANES + count, count), F32),
             pltpu.VMEM((n_tm, own, width), F32),
             pltpu.VMEM((n_tm, own, width), F32),
             dma((2,)),

time: 35 us -> 36.4 us (1.040)
  Pallas kernels: 34.2 us -> 35.6 us
    pallas_call x1, Pallas kernels: 34.2 us -> 35.6 us  [on_device(): pl.pallas_call(functools.partial(kernel, n_tm, n_tr), out_shape=pltpu.VME...]
where the time goes in v4:
time: 36.4 us; the launch traced here: 36.2 us
  Pallas kernels  35.6 us (98%)
  other arithmetic  0.63 us (2%)
    pallas_call x1, Pallas kernels, on_device(): pl.pallas_call(functools.partial(kernel, n_tm, n_tr), out_shape=pltpu.VME...  35.6 us

profile of v4, /device:TPU:0, one launch (start us, length us, event | category | flops | bytes accessed | tf_op | source)
XLA Modules:
  0.0 36.2 jit_solution(11503644231589799946)
XLA Ops:
  0.0 0.0 copy-start
  0.0 0.0 copy-start.1
  0.0 35.6 %shard_map.37 = f32[16,512]{1,0:T(8,128)S(1)} custom-call(bf16[16,512]{1,0:T(8,128)(2,1)} %observed.1, s32[16,512]{1,0:T(8,128)} %sampled.1, bf16[2,2048,128]{2,1,0:T(8,128)(2,1)} %bitcast.1), custom_call_target="tpu_custom_call" | custom-call | flops 2000000000 | bytes 2000000 | tf_op jit(solution)/shard_map/pallas_call | solution.py:338
  35.6 0.0 copy-done
  35.6 0.0 copy-done.1
  35.6 0.6 %divide_select_fusion = f32[16,512]{1,0:T(8,128)} fusion(f32[16,512]{1,0:T(8,128)S(1)} %shard_map.37, bf16[16,512]{1,0:T(8,128)(2,1)S(1)} %copy-done.1, s32[16,512]{1,0:T(8,128)S(1)} %copy-done, f32[512]{0:T(512)S(1)} %minimum_convert_fusion), kind=kLoop, calls=%fused_computation | loop fusion | flops 32768 | bytes 116736 | tf_op jit(solution)/shard_map/jit(_where)/select_n | solution.py:375
  (1 shorter events, 0.0 us)
Async XLA Ops:
  0.0 35.6 %copy-start = (s32[16,512]{1,0:T(8,128)S(1)}, s32[16,512]{1,0:T(8,128)}, u32[]{:S(2)}) copy-start(s32[16,512]{1,0:T(8,128)} %sampled.1) | copy-start | bytes 98308
  0.0 35.6 %copy-start.1 = (bf16[16,512]{1,0:T(8,128)(2,1)S(1)}, bf16[16,512]{1,0:T(8,128)(2,1)}, u32[]{:S(2)}) copy-start(bf16[16,512]{1,0:T(8,128)(2,1)} %observed.1) | copy-start | bytes 49156

commit v5 on v3

--- a/solution.py
+++ b/solution.py
@@ -127,6 +127,10 @@
     data[...] = masked.astype(BF)
     for i in range(n_tm):
         slices[i] = masked[own * i : own * (i + 1)]
+    fetch.wait()
+    with jax.named_scope("probes_transposed"):
+        for g in range(groups):
+            probes_t[probe_count * g : probe_count * (g + 1), :] = probes[g].T
     pl.semaphore_wait(barrier, n_tm + n_tr - 2)
 
     pending = []
@@ -140,11 +144,6 @@
         c.start()
         pending.append(c)
     windows[tm] = slices[tm]
-
-    fetch.wait()
-    with jax.named_scope("probes_transposed"):
-        for g in range(groups):
-            probes_t[probe_count * g : probe_count * (g + 1), :] = probes[g].T
 
     halo_copy.wait_recv()
     with jax.named_scope("sketch_part"):

time: 35 us -> 34.9 us (level)
  no operation moved by 1% of the time
where the time goes in v5:
time: 34.9 us; the launch traced here: 34.7 us
  Pallas kernels  34 us (97%)
  other arithmetic  0.63 us (2%)
    pallas_call x1, Pallas kernels, on_device(): pl.pallas_call(functools.partial(kernel, n_tm, n_tr), out_shape=pltpu.VME...  34 us

profile of v5, /device:TPU:0, one launch (start us, length us, event | category | flops | bytes accessed | tf_op | source)
XLA Modules:
  0.0 34.7 jit_solution(10029798954196664603)
XLA Ops:
  0.0 0.0 copy-start
  0.0 0.0 copy-start.1
  0.0 34.0 %shard_map.37 = f32[16,512]{1,0:T(8,128)S(1)} custom-call(bf16[16,512]{1,0:T(8,128)(2,1)} %observed.1, s32[16,512]{1,0:T(8,128)} %sampled.1, bf16[2,2048,128]{2,1,0:T(8,128)(2,1)} %bitcast.1), custom_call_target="tpu_custom_call" | custom-call | flops 2000000000 | bytes 2000000 | tf_op jit(solution)/shard_map/pallas_call | solution.py:331
  34.0 0.0 copy-done
  34.0 0.0 copy-done.1
  34.0 0.6 %divide_select_fusion = f32[16,512]{1,0:T(8,128)} fusion(f32[16,512]{1,0:T(8,128)S(1)} %shard_map.37, bf16[16,512]{1,0:T(8,128)(2,1)S(1)} %copy-done.1, s32[16,512]{1,0:T(8,128)S(1)} %copy-done, f32[512]{0:T(512)S(1)} %minimum_convert_fusion), kind=kLoop, calls=%fused_computation | loop fusion | flops 32768 | bytes 116736 | tf_op jit(solution)/shard_map/jit(_where)/select_n | solution.py:368
  (1 shorter events, 0.0 us)
Async XLA Ops:
  0.0 34.0 %copy-start = (s32[16,512]{1,0:T(8,128)S(1)}, s32[16,512]{1,0:T(8,128)}, u32[]{:S(2)}) copy-start(s32[16,512]{1,0:T(8,128)} %sampled.1) | copy-start | bytes 98308
  0.0 34.0 %copy-start.1 = (bf16[16,512]{1,0:T(8,128)(2,1)S(1)}, bf16[16,512]{1,0:T(8,128)(2,1)}, u32[]{:S(2)}) copy-start(bf16[16,512]{1,0:T(8,128)(2,1)} %observed.1) | copy-start | bytes 49156
